TPU v7x, 32 devices: a whole 2x2x4 slice. The times are simulated.
32 devices in a mesh: atoms: 8 (over y, x, core), chan: 4 (over z).
Axes of the slice: x: 2, y: 2, z: 4, core: 2. Of those that a mesh axis runs over, the one named last changes fastest.
Arguments:
- features: bfloat16 [16384, 512], P('atoms', 'chan'), may hold values from -6 to 6
- positions: int32 [3, 16384], P(None, 'atoms'), may hold values from 0 to 4095
- wavevectors: int32 [3, 2048], replicated, may hold values from -8 to 8
- radial_weight: float32 [16, 512], P(None, 'chan'), may hold values from -6 to 6
- weight_in: bfloat16 [512, 1024], replicated, may hold values from -0.25 to 0.25
- weight_out: bfloat16 [1024, 512], replicated, may hold values from -0.1875 to 0.1875
- cotangent: bfloat16 [16384, 512], P('atoms', 'chan'), may hold values from -6 to 6
Outputs:
- output: bfloat16 [16384, 512], P('atoms', 'chan')
- feature_grad: float32 [16384, 512], P('atoms', 'chan')
All inputs are finite; a program needn't handle non-finite values.
Results may differ from a plain program's by a relative error of at most 0.0057.
Values may be sent and summed in bfloat16 or wider, within the bound.
A program may use at most 128 MiB of HBM per device.

v0:
```python
import math

import jax
import jax.numpy as jnp
from jax import lax
from jax.sharding import PartitionSpec as P

NB = 16
KMAX = 8
GRID = 4096


def phase_rows(wavevectors, places):
    product = wavevectors[0][:, None] * places[0][None, :]
    product = product + wavevectors[1][:, None] * places[1][None, :]
    product = product + wavevectors[2][:, None] * places[2][None, :]
    remain = jnp.mod(product, GRID)
    angles = remain.astype(jnp.float32) * (2.0 * math.pi / GRID)
    return jnp.concatenate([jnp.cos(angles), jnp.sin(angles)], 0).astype(jnp.bfloat16)


def radial_filter(wavevectors, radial_weight, atom_count):
    lengths = jnp.sqrt(jnp.sum((wavevectors * wavevectors).astype(jnp.float32), 0))
    spacing = KMAX * math.sqrt(3.0) / (NB - 1)
    centers = jnp.arange(NB).astype(jnp.float32) * spacing
    basis = jnp.exp(-0.5 * ((lengths[:, None] - centers[None, :]) / spacing) ** 2)
    filt = jnp.dot(
        basis, radial_weight, precision=lax.Precision.HIGHEST, preferred_element_type=jnp.float32
    )
    filt = filt * (2.0 * wavevectors.shape[1] * atom_count) ** (-0.5)
    return jnp.concatenate([filt, filt], 0)


def shards(features, positions, wavevectors, radial_weight, weight_in, weight_out, cotangent):
    local_atoms = features.shape[0]
    atom_count = local_atoms * lax.axis_size("atoms")
    phases = phase_rows(wavevectors, positions)
    filt2 = radial_filter(wavevectors, radial_weight, atom_count)

    def ewald(field):
        partial_value = jnp.dot(phases, field, preferred_element_type=jnp.float32)
        totals = lax.psum(partial_value, "atoms")
        shaped = (filt2 * totals).astype(jnp.bfloat16)
        return lax.dot_general(
            phases, shaped, (((0,), (0,)), ((), ())), preferred_element_type=jnp.float32
        )

    message = ewald(features).astype(jnp.bfloat16)
    row_message, row_cotangent = (
        lax.all_to_all(message, "chan", split_axis=0, concat_axis=1, tiled=True),
        lax.all_to_all(cotangent, "chan", split_axis=0, concat_axis=1, tiled=True),
    )
    message_f = row_message.astype(jnp.float32)
    scale = jnp.sqrt(jnp.mean(message_f * message_f, -1, keepdims=True) + 1e-06)
    unit = message_f / scale
    normed = unit.astype(jnp.bfloat16)
    pre = jnp.dot(normed, weight_in, preferred_element_type=jnp.float32)
    hidden = jax.nn.silu(pre).astype(jnp.bfloat16)
    update = jnp.dot(hidden, weight_out, preferred_element_type=jnp.float32).astype(jnp.bfloat16)
    g_hidden = lax.dot_general(
        row_cotangent, weight_out, (((1,), (1,)), ((), ())), preferred_element_type=jnp.float32
    )
    sigmoid_pre = jax.nn.sigmoid(pre)
    g_pre = (g_hidden * sigmoid_pre * (1.0 + pre * (1.0 - sigmoid_pre))).astype(jnp.bfloat16)
    g_normed = lax.dot_general(
        g_pre, weight_in, (((1,), (1,)), ((), ())), preferred_element_type=jnp.float32
    )
    g_message = ((g_normed - unit * jnp.mean(g_normed * unit, -1, keepdims=True)) / scale).astype(
        jnp.bfloat16
    )
    chan_update, chan_gradient = (
        lax.all_to_all(update, "chan", split_axis=1, concat_axis=0, tiled=True),
        lax.all_to_all(g_message, "chan", split_axis=1, concat_axis=0, tiled=True),
    )
    output = (features.astype(jnp.float32) + chan_update.astype(jnp.float32)).astype(jnp.bfloat16)
    feature_grad = cotangent.astype(jnp.float32) + ewald(chan_gradient)
    return (output, feature_grad)


def solution(mesh):
    placed = (
        P("atoms", "chan"),
        P(None, "atoms"),
        P(),
        P(None, "chan"),
        P(),
        P(),
        P("atoms", "chan"),
    )
    return jax.shard_map(
        shards,
        mesh=mesh,
        in_specs=placed,
        out_specs=(P("atoms", "chan"), P("atoms", "chan")),
        check_vma=False,
    )
```

profile of v0, /device:TPU:0, one launch (start us, length us, event | category | flops | bytes accessed | tf_op | source)
XLA Modules:
  0.0 307.7 jit_solution(10255565296844197323)
XLA Ops:
  7.2 0.0 copy-start
  7.2 0.0 all-reduce.3.cloned.1.call-start
  7.2 0.9 fusion.33
  8.1 0.9 fusion.32
  9.0 0.0 copy-start.3
  9.0 72.1 %cosine_convert_fusion = (bf16[2048,2048]{1,0:T(8,128)(2,1)S(1)}, bf16[2048,2048]{1,0:T(8,128)(2,1)}) fusion(s32[2048]{0:T(1024)S(1)} %bitcast.41, s32[2048]{0:T(1024)S(1)} %bitcast.45, s32[2048]{0:T(1024)S(1)} %bitcast.42, s32[2048]{0:T(1024)S(1)} %bitcast.44, s32[2048]{0:T(1024)S(1)} %bitcast.40, s32[2048]{0:T(1024)S(1)} %bitcast.43), kind=kLoop, calls=%fused_computation.8 | loop fusion | flops 83886080 | bytes 16826368 | tf_op jit(solution)/shard_map/convert.4
  81.2 0.0 copy-start.1
  81.2 3.2 %copy-done.1 = bf16[2048,2048]{1,0:T(8,128)(2,1)} copy-done((bf16[2048,2048]{1,0:T(8,128)(2,1)}, bf16[2048,2048]{1,0:T(8,128)(2,1)S(1)}, u32[]{:S(2)}) %copy-start.1) | copy-done | bytes 8388632
  84.4 0.0 copy-done.3
  84.4 0.0 copy-start.4
  84.4 0.0 copy-start.5
  84.4 9.3 %fusion.31 = f32[4096,128]{1,0:T(8,128)} fusion(bf16[2048,128]{1,0:T(8,128)(2,1)S(1)} %copy-done.3, bf16[2048,2048]{1,0:T(8,128)(2,1)} %get-tuple-element.3, bf16[2048,2048]{1,0:T(8,128)(2,1)S(1)} %get-tuple-element.2), kind=kOutput, calls=%fused_computation.54 | convolution fusion | flops 2181038080 | bytes 19398656 | tf_op jit(solution)/shard_map/dot_general | solution.py:41
  93.7 0.0 all-reduce.3.cloned.1.call-update
  93.7 6.3 %all-to-all-start.2 = ((bf16[4,512,128]{2,1,0:T(8,128)(2,1)}), bf16[4,512,128]{2,1,0:T(8,128)(2,1)S(1)}, u32[]{:S(2)}, u32[]{:S(2)}) async-start(bf16[4,512,128]{2,1,0:T(8,128)(2,1)} %bitcast.12), calls=%async_computation.2 | async-start | bytes 1048576 | tf_op jit(solution)/shard_map/all_to_all | solution.py:51
  100.0 0.0 copy-done.4
  100.1 0.0 copy-done.5
  100.1 1.9 convolution_multiply_fusion
  102.0 0.0 copy-start.2
  102.0 56.0 %all-reduce.3.cloned.1.call-done = f32[4096,128]{1,0:T(8,128)} async-done(((f32[4096,128]{1,0:T(8,128)}), f32[4096,128]{1,0:T(8,128)}) %all-reduce.3.cloned.1.call-update) | async-done | bytes 2097168 | tf_op jit(solution)/shard_map/psum | solution.py:42
  158.0 9.6 %convolution_convert_fusion = bf16[2048,128]{1,0:T(8,128)(2,1)} fusion(f32[4096,128]{1,0:T(8,128)} %all-reduce.3.cloned.1.call-done, f32[2048,128]{1,0:T(8,128)S(1)} %convolution_multiply_fusion, bf16[2048,2048]{1,0:T(8,128)(2,1)} %get-tuple-element.3, bf16[2048,2048]{1,0:T(8,128)(2,1)} %copy-done.1), kind=kOutput, calls=%fused_computation.10 | convolution fusion | flops 2182873088 | bytes 20447232 | tf_op jit(solution)/shard_map/dot_general | solution.py:44
  167.6 0.0 copy-done.2
  167.6 0.0 all-to-all-done.2
  167.6 4.6 %all-to-all-start = ((bf16[4,512,128]{2,1,0:T(8,128)(2,1)}), bf16[4,512,128]{2,1,0:T(8,128)(2,1)S(1)}, u32[]{:S(2)}, u32[]{:S(2)}) async-start(bf16[4,512,128]{2,1,0:T(8,128)(2,1)} %bitcast.39), calls=%async_computation | async-start | bytes 1048576 | tf_op jit(solution)/shard_map/all_to_all | solution.py:50
  172.2 1.0 copy.20
  173.2 12.4 %all-to-all-done = bf16[4,512,128]{2,1,0:T(8,128)(2,1)S(1)} async-done(((bf16[4,512,128]{2,1,0:T(8,128)(2,1)}), bf16[4,512,128]{2,1,0:T(8,128)(2,1)S(1)}, u32[]{:S(2)}, u32[]{:S(2)}) %all-to-all-start) | async-done | bytes 524320 | tf_op jit(solution)/shard_map/all_to_all | solution.py:50
  185.6 0.2 fusion.8
  185.8 0.1 convert_bitcast_fusion
  185.9 0.3 copy.18
  186.2 0.1 bitcast_divide_fusion
  186.4 0.0 copy-done
  186.4 2.1 fusion.13
  188.5 4.6 %multiply_reduce_fusion = (f32[512]{0:T(512)S(1)}, f32[512,512]{0,1:T(8,128)}) fusion(f32[512,512]{0,1:T(8,128)S(1)} %bitcast_divide_fusion, bf16[512,1024]{1,0:T(8,128)(2,1)S(1)} %copy-done, f32[512,1024]{1,0:T(8,128)} %fusion.13, bf16[512,512]{0,1:T(8,128)(2,1)} %bitcast.38, bf16[1024,512]{1,0:T(8,128)(2,1)} %param.12), kind=kOutput, calls=%fused_computation.30 | convolution fusion | flops 1078984192 | bytes 6817792 | tf_op jit(solution)/shard_map/dot_general | solution.py:65
  193.1 1.4 divide_convert_fusion
  194.5 1.0 copy.21
  195.5 3.5 %all-to-all-start.3 = ((bf16[512,4,128]{2,0,1:T(8,128)(2,1)}), bf16[512,4,128]{2,0,1:T(8,128)(2,1)S(1)}, u32[]{:S(2)}, u32[]{:S(2)}) async-start(bf16[512,4,128]{2,0,1:T(8,128)(2,1)} %copy.21), calls=%async_computation.3 | async-start | bytes 1048576 | tf_op jit(solution)/shard_map/all_to_all | solution.py:73
  199.0 3.5 %convolution_convert_fusion.1 = bf16[512,512]{0,1:T(8,128)(2,1)} fusion(bf16[1024,512]{1,0:T(8,128)(2,1)} %param.12, f32[512,1024]{1,0:T(8,128)} %fusion.13), kind=kOutput, calls=%fused_computation.22 | convolution fusion | flops 539754496 | bytes 3670016 | tf_op jit(solution)/shard_map/dot_general | solution.py:59
  202.5 10.3 %all-to-all-done.3 = bf16[512,4,128]{2,0,1:T(8,128)(2,1)S(1)} async-done(((bf16[512,4,128]{2,0,1:T(8,128)(2,1)}), bf16[512,4,128]{2,0,1:T(8,128)(2,1)S(1)}, u32[]{:S(2)}, u32[]{:S(2)}) %all-to-all-start.3) | async-done | bytes 524320 | tf_op jit(solution)/shard_map/all_to_all | solution.py:73
  212.9 3.5 %all-to-all-start.1 = ((bf16[512,4,128]{0,2,1:T(8,128)(2,1)}), bf16[512,4,128]{0,2,1:T(8,128)(2,1)S(1)}, u32[]{:S(2)}, u32[]{:S(2)}) async-start(bf16[512,4,128]{0,2,1:T(8,128)(2,1)} %bitcast.9), calls=%async_computation.1 | async-start | bytes 1048576 | tf_op jit(solution)/shard_map/all_to_all | solution.py:72
  216.3 0.3 all-reduce.5.cloned.1.call-start
  216.6 9.8 %fusion.30 = f32[4096,128]{1,0:T(8,128)} fusion(bf16[2048,128]{1,0:T(8,128)(2,1)S(1)} %bitcast.37, bf16[2048,2048]{1,0:T(8,128)(2,1)} %get-tuple-element.3, bf16[2048,2048]{1,0:T(8,128)(2,1)} %copy-done.1), kind=kOutput, calls=%fused_computation.53 | convolution fusion | flops 2181038080 | bytes 19398656 | tf_op jit(solution)/shard_map/dot_general | solution.py:41
  226.4 0.0 all-reduce.5.cloned.1.call-update
  226.4 3.9 %all-to-all-done.1 = bf16[512,4,128]{0,2,1:T(8,128)(2,1)S(1)} async-done(((bf16[512,4,128]{0,2,1:T(8,128)(2,1)}), bf16[512,4,128]{0,2,1:T(8,128)(2,1)S(1)}, u32[]{:S(2)}, u32[]{:S(2)}) %all-to-all-start.1) | async-done | bytes 524320 | tf_op jit(solution)/shard_map/all_to_all | solution.py:72
  230.3 0.1 convert_bitcast_fusion.1
  230.4 0.3 copy.19
  230.8 2.1 fusion.11
  232.8 55.5 %all-reduce.5.cloned.1.call-done = f32[4096,128]{1,0:T(8,128)} async-done(((f32[4096,128]{1,0:T(8,128)}), f32[4096,128]{1,0:T(8,128)}) %all-reduce.5.cloned.1.call-update) | async-done | bytes 2097168 | tf_op jit(solution)/shard_map/psum | solution.py:42
  288.3 12.6 %convolution_add_fusion = f32[2048,128]{1,0:T(8,128)} fusion(f32[4096,128]{1,0:T(8,128)} %all-reduce.5.cloned.1.call-done, f32[2048,128]{1,0:T(8,128)} %copy-done.2, bf16[2048,128]{1,0:T(8,128)(2,1)} %param.13, bf16[2048,2048]{1,0:T(8,128)(2,1)} %get-tuple-element.3, bf16[2048,2048]{1,0:T(8,128)(2,1)} %copy-done.1), kind=kOutput, calls=%fused_computation.11 | convolution fusion | flops 2183135232 | bytes 21495808 | tf_op jit(solution)/shard_map/dot_general | solution.py:44
  (5 shorter events, 0.1 us)
Async XLA Ops:
  7.2 179.2 %copy-start = (bf16[512,1024]{1,0:T(8,128)(2,1)S(1)}, bf16[512,1024]{1,0:T(8,128)(2,1)}, u32[]{:S(2)}) copy-start(bf16[512,1024]{1,0:T(8,128)(2,1)} %param.11) | copy-start | bytes 3145732
  7.2 150.8 %all-reduce.3.cloned.1.call-start = ((), (), s32[]{:S(2)}) async-start(), calls=%async_computation.4 | async-start | bytes 4194304 | tf_op jit(solution)/shard_map/psum | solution.py:42
  9.0 75.4 %copy-start.3 = (bf16[2048,128]{1,0:T(8,128)(2,1)S(1)}, bf16[2048,128]{1,0:T(8,128)(2,1)}, u32[]{:S(2)}) copy-start(bf16[2048,128]{1,0:T(8,128)(2,1)} %param.7) | copy-start | bytes 1572868
  81.2 3.2 %copy-start.1 = (bf16[2048,2048]{1,0:T(8,128)(2,1)}, bf16[2048,2048]{1,0:T(8,128)(2,1)S(1)}, u32[]{:S(2)}) copy-start(bf16[2048,2048]{1,0:T(8,128)(2,1)S(1)} %get-tuple-element.2) | copy-start | bytes 25165828
  84.4 15.6 %copy-start.4 = (s32[3,2048]{1,0:T(4,128)S(1)}, s32[3,2048]{1,0:T(4,128)}, u32[]{:S(2)}) copy-start(s32[3,2048]{1,0:T(4,128)} %param.9) | copy-start | bytes 73732
  84.4 15.7 %copy-start.5 = (f32[16,128]{1,0:T(8,128)S(1)}, f32[16,128]{1,0:T(8,128)}, u32[]{:S(2)}) copy-start(f32[16,128]{1,0:T(8,128)} %param.10) | copy-start | bytes 24580
  93.7 73.9 %all-to-all-start.2 = ((bf16[4,512,128]{2,1,0:T(8,128)(2,1)}), bf16[4,512,128]{2,1,0:T(8,128)(2,1)S(1)}, u32[]{:S(2)}, u32[]{:S(2)}) async-start(bf16[4,512,128]{2,1,0:T(8,128)(2,1)} %bitcast.12), calls=%async_computation.2 | async-start | bytes 1048576 | tf_op jit(solution)/shard_map/all_to_all | solution.py:51
  102.0 65.6 %copy-start.2 = (f32[2048,128]{1,0:T(8,128)}, f32[2048,128]{1,0:T(8,128)S(1)}, u32[]{:S(2)}) copy-start(f32[2048,128]{1,0:T(8,128)S(1)} %convolution_multiply_fusion) | copy-start | bytes 3145732
  167.6 18.1 %all-to-all-start = ((bf16[4,512,128]{2,1,0:T(8,128)(2,1)}), bf16[4,512,128]{2,1,0:T(8,128)(2,1)S(1)}, u32[]{:S(2)}, u32[]{:S(2)}) async-start(bf16[4,512,128]{2,1,0:T(8,128)(2,1)} %bitcast.39), calls=%async_computation | async-start | bytes 1048576 | tf_op jit(solution)/shard_map/all_to_all | solution.py:50
  195.5 17.4 %all-to-all-start.3 = ((bf16[512,4,128]{2,0,1:T(8,128)(2,1)}), bf16[512,4,128]{2,0,1:T(8,128)(2,1)S(1)}, u32[]{:S(2)}, u32[]{:S(2)}) async-start(bf16[512,4,128]{2,0,1:T(8,128)(2,1)} %copy.21), calls=%async_computation.3 | async-start | bytes 1048576 | tf_op jit(solution)/shard_map/all_to_all | solution.py:73
  212.9 17.4 %all-to-all-start.1 = ((bf16[512,4,128]{0,2,1:T(8,128)(2,1)}), bf16[512,4,128]{0,2,1:T(8,128)(2,1)S(1)}, u32[]{:S(2)}, u32[]{:S(2)}) async-start(bf16[512,4,128]{0,2,1:T(8,128)(2,1)} %bitcast.9), calls=%async_computation.1 | async-start | bytes 1048576 | tf_op jit(solution)/shard_map/all_to_all | solution.py:72
  216.3 72.0 %all-reduce.5.cloned.1.call-start = ((), (), s32[]{:S(2)}) async-start(), calls=%async_computation.5 | async-start | bytes 4194304 | tf_op jit(solution)/shard_map/psum | solution.py:42
Sparse Core Ops, SparseCore 0:
  93.8 64.1 all-reduce.2
  226.6 61.7 all-reduce.4
where the time goes:
time: 308 us
  waiting for transfers between devices  138 us (45%)
  other arithmetic  76.1 us (25%)
  matrix products  53.3 us (17%)
  starting transfers between devices  18.2 us (6%)
  between operations  14.2 us (5%)
  local copies, waits for them, and re-layouts  7.73 us (3%)
    psum x2, waiting for transfers between devices, ewald(): totals = lax.psum(partial_value, 'atoms')  112 us
    another operation x1, other arithmetic  72.1 us
    dot_general x2, matrix products, ewald(): lax.dot_general(phases, shaped, (((0,), (0,)), ((), ())), preferred_eleme...  22.1 us
    dot_general x2, matrix products, ewald(): partial_value = jnp.dot(phases, field, preferred_element_type=jnp.float32)  19.1 us
    all_to_all x1, waiting for transfers between devices, shards(): lax.all_to_all(message, 'chan', split_axis=0, concat_axis=1, tiled=True)  12.4 us
    all_to_all x1, waiting for transfers between devices, shards(): lax.all_to_all(g_message, 'chan', split_axis=1, concat_axis=0, tiled=True)  10.3 us
    all_to_all x1, starting transfers between devices, shards(): lax.all_to_all(cotangent, 'chan', split_axis=0, concat_axis=1, tiled=True)  6.33 us
  transfers between devices with their start and end apart: 6, of which 5 were waited for; matrix products, arithmetic and copies ran while one was open for 9% of the time, Pallas kernels for 0%

commit v1 on v0

v1 whole, which is shorter than its diff:
```python
import functools
import math

import jax
import jax.numpy as jnp
import numpy as np
from jax import lax
from jax.experimental import pallas as pl
from jax.experimental.pallas import tpu as pltpu
from jax.sharding import PartitionSpec as P

NB = 16
KMAX = 8
GRID = 4096
MESH = pl.DeviceIdType.MESH
BLOCK = 128


def fit_even(fn, degree):
    cheb = np.polynomial.chebyshev.Chebyshev.interpolate(
        lambda u: fn(np.sqrt(u)), degree, domain=[0.0, 0.25]
    )
    return [float(v) for v in cheb.convert(kind=np.polynomial.Polynomial, domain=[-1, 1], window=[-1, 1]).coef]


def sin_over(f):
    return math.sqrt(2.0) * math.pi * np.sinc(f)


def cos_half(f):
    return math.sqrt(2.0) * np.cos(math.pi * f)


SIN_COEF = fit_even(sin_over, 3)
COS_COEF = fit_even(cos_half, 3)


def horner(coef, u):
    total = coef[-1] * u + coef[-2]
    for c in coef[-3::-1]:
        total = total * u + c
    return total


def ewald_kernel(first, n, chunks, *refs):
    if first:
        (wave_ref, place_ref, x_ref, filt_ref, out_ref, phases_out,
         ph, part, rs_src, rs_dst, ag, acc, local_sem, rs_send, rs_recv, ag_send, ag_recv) = refs
    else:
        (phases_in, x_ref, filt_ref, cot_ref, out_ref,
         ph, part, rs_src, rs_dst, ag, acc, local_sem, rs_send, rs_recv, ag_send, ag_recv) = refs
    me = lax.axis_index("atoms")
    atoms = x_ref.shape[0]
    rows = n * BLOCK
    waves = rows // 2

    def local_copy(j):
        span = pl.ds(j * rows, rows)
        if first:
            return pltpu.make_async_copy(ph.at[span], phases_out.at[span], local_sem.at[j])
        return pltpu.make_async_copy(phases_in.at[span], ph.at[span], local_sem.at[j])

    if not first:
        for j in range(chunks):
            local_copy(j).start()

    barrier = pltpu.get_barrier_semaphore()

    def greet(step, carry):
        pl.semaphore_signal(
            barrier, inc=1, device_id={"atoms": lax.rem(me + step, n)}, device_id_type=MESH
        )
        return carry

    lax.fori_loop(1, n, greet, 0)

    def rs_copy(j, here, there):
        return pltpu.make_async_remote_copy(
            src_ref=rs_src.at[j, there],
            dst_ref=rs_dst.at[j, here],
            send_sem=rs_send.at[j, there],
            recv_sem=rs_recv.at[j, here],
            device_id={"atoms": there},
            device_id_type=MESH,
        )

    def ag_copy(j, owner, there):
        return pltpu.make_async_remote_copy(
            src_ref=ag.at[j, owner],
            dst_ref=ag.at[j, owner],
            send_sem=ag_send.at[j, there],
            recv_sem=ag_recv.at[j, owner],
            device_id={"atoms": there},
            device_id_type=MESH,
        )

    def peers(fn):
        def body(step, carry):
            fn(lax.rem(me + step, n))
            return carry

        lax.fori_loop(1, n, body, 0)

    tile = min(256, atoms)

    def generate(j):
        top = j * rows

        def body(a, carry):
            cols = pl.ds(pl.multiple_of(a * tile, tile), tile)
            turns = jnp.dot(
                wave_ref[pl.ds(j * waves, waves), :], place_ref[:, cols],
                preferred_element_type=jnp.float32,
            )
            f = turns - jnp.round(turns)
            u = f * f
            s = f * horner(SIN_COEF, u)
            c = horner(COS_COEF, u)
            ph[pl.ds(top, waves), cols] = (1.0 - s * s).astype(jnp.bfloat16)
            ph[pl.ds(top + waves, waves), cols] = (s * c).astype(jnp.bfloat16)
            return carry

        lax.fori_loop(0, atoms // tile, body, 0)

    group = min(4, n)

    def project(j):
        def body(i, carry):
            span = pl.ds(pl.multiple_of(j * rows + i * (group * BLOCK), group * BLOCK), group * BLOCK)
            value = jnp.dot(ph[span, :], x_ref[...], preferred_element_type=jnp.float32)
            value = value.reshape(group, BLOCK, value.shape[-1])
            slots = pl.ds(i * group, group)
            part[j, slots] = value
            rs_src[j, slots] = value.astype(jnp.bfloat16)
            return carry

        lax.fori_loop(0, n // group, body, 0)

    def reduce(j):
        part_own = part[j, me]

        def body(step, total):
            peer = lax.rem(me + step, n)
            rs_copy(j, peer, me).wait_recv()
            return total + rs_dst[j, peer].astype(jnp.float32)

        total = lax.fori_loop(1, n, body, part_own)
        shaped = filt_ref[pl.ds(j * BLOCK, BLOCK), :] * total
        ag[j, me] = shaped.T.astype(jnp.bfloat16)
        peers(lambda peer: ag_copy(j, me, peer).start())

    wide = min(512, atoms)

    def back(j):
        peers(lambda peer: ag_copy(j, peer, me).wait_recv())
        lhs = jnp.concatenate([ag[j, d] for d in range(n)], axis=1)

        def body(a, carry):
            cols = pl.ds(pl.multiple_of(a * wide, wide), wide)
            value = jnp.dot(lhs, ph[pl.ds(j * rows, rows), cols], preferred_element_type=jnp.float32)
            if j > 0:
                value = value + acc[:, cols]
            if j < chunks - 1:
                acc[:, cols] = value
            elif first:
                out_ref[cols, :] = value.T.astype(jnp.bfloat16)
            else:
                out_ref[cols, :] = cot_ref[cols, :].astype(jnp.float32) + value.T
            return carry

        lax.fori_loop(0, atoms // wide, body, 0)

    for j in range(chunks + 2):
        if j < chunks:
            if first:
                generate(j)
                local_copy(j).start()
            else:
                local_copy(j).wait()
            project(j)
            if j == 0:
                pl.semaphore_wait(barrier, n - 1)
            peers(lambda peer: rs_copy(j, me, peer).start())
        if 1 <= j <= chunks:
            reduce(j - 1)
        if j >= 2:
            back(j - 2)

    for j in range(chunks):
        if first:
            local_copy(j).wait()
        peers(lambda peer: rs_copy(j, me, peer).wait_send())
        peers(lambda peer: ag_copy(j, me, peer).wait_send())


def ewald(first, n, total_rows, *operands):
    field = operands[2] if first else operands[1]
    atoms, channels = field.shape
    chunks = total_rows // (n * BLOCK)
    vmem = pl.BlockSpec(memory_space=pltpu.VMEM)
    anywhere = pl.BlockSpec(memory_space=pl.ANY)
    if first:
        in_specs = [vmem] * 4
        out_shape = (
            jax.ShapeDtypeStruct((atoms, channels), jnp.bfloat16),
            jax.ShapeDtypeStruct((total_rows, atoms), jnp.bfloat16),
        )
        out_specs = (vmem, anywhere)
    else:
        in_specs = [anywhere] + [vmem] * 3
        out_shape = jax.ShapeDtypeStruct((atoms, channels), jnp.float32)
        out_specs = vmem
    block = (chunks, n, BLOCK, channels)
    sems = pltpu.SemaphoreType.DMA((chunks, n))
    return pl.pallas_call(
        functools.partial(ewald_kernel, first, n, chunks),
        out_shape=out_shape,
        in_specs=in_specs,
        out_specs=out_specs,
        scratch_shapes=[
            pltpu.VMEM((total_rows, atoms), jnp.bfloat16),
            pltpu.VMEM(block, jnp.float32),
            pltpu.VMEM(block, jnp.bfloat16),
            pltpu.VMEM(block, jnp.bfloat16),
            pltpu.VMEM((chunks, n, channels, BLOCK), jnp.bfloat16),
            pltpu.VMEM((channels, atoms), jnp.float32),
            pltpu.SemaphoreType.DMA((chunks,)),
            sems, sems, sems, sems,
        ],
        compiler_params=pltpu.CompilerParams(
            collective_id=0 if first else 1, has_side_effects=True, vmem_limit_bytes=44 * 2**20
        ),
        name="ewald_first" if first else "ewald_second",
    )(*operands)


def own_filter(wavevectors, radial_weight, atom_count, n, me):
    kvec = wavevectors.shape[1]
    waves = n * BLOCK // 2
    chunked = wavevectors.reshape(3, kvec // waves, n // 2, BLOCK)
    own = lax.dynamic_index_in_dim(chunked, lax.rem(me, n // 2), 2, keepdims=False).reshape(3, -1)
    lengths = jnp.sqrt(jnp.sum((own * own).astype(jnp.float32), 0))
    spacing = KMAX * math.sqrt(3.0) / (NB - 1)
    centers = jnp.arange(NB).astype(jnp.float32) * spacing
    basis = jnp.exp(-0.5 * ((lengths[:, None] - centers[None, :]) / spacing) ** 2)
    filt = jnp.dot(
        basis, radial_weight, precision=lax.Precision.HIGHEST, preferred_element_type=jnp.float32
    )
    return filt * (2.0 * kvec * atom_count) ** (-0.5)


def shards(features, positions, wavevectors, radial_weight, weight_in, weight_out, cotangent):
    local_atoms = features.shape[0]
    n = lax.axis_size("atoms")
    atom_count = local_atoms * n
    total_rows = 2 * wavevectors.shape[1]
    filt = own_filter(wavevectors, radial_weight, atom_count, n, lax.axis_index("atoms"))

    wave = wavevectors.T.astype(jnp.float32)
    wave = jnp.concatenate([wave * (64.0 / GRID), wave * (1.0 / GRID)], 1)
    wave = jnp.pad(wave, ((0, 0), (0, 10))).astype(jnp.bfloat16)
    place = jnp.concatenate([positions // 64, positions % 64], 0)
    place = jnp.pad(place, ((0, 10), (0, 0))).astype(jnp.bfloat16)

    message, phases = ewald(True, n, total_rows, wave, place, features, filt)
    row_message, row_cotangent = (
        lax.all_to_all(message, "chan", split_axis=0, concat_axis=1, tiled=True),
        lax.all_to_all(cotangent, "chan", split_axis=0, concat_axis=1, tiled=True),
    )
    message_f = row_message.astype(jnp.float32)
    scale = jnp.sqrt(jnp.mean(message_f * message_f, -1, keepdims=True) + 1e-06)
    unit = message_f / scale
    normed = unit.astype(jnp.bfloat16)
    pre = jnp.dot(normed, weight_in, preferred_element_type=jnp.float32)
    hidden = jax.nn.silu(pre).astype(jnp.bfloat16)
    update = jnp.dot(hidden, weight_out, preferred_element_type=jnp.float32).astype(jnp.bfloat16)
    g_hidden = lax.dot_general(
        row_cotangent, weight_out, (((1,), (1,)), ((), ())), preferred_element_type=jnp.float32
    )
    sigmoid_pre = jax.nn.sigmoid(pre)
    g_pre = (g_hidden * sigmoid_pre * (1.0 + pre * (1.0 - sigmoid_pre))).astype(jnp.bfloat16)
    g_normed = lax.dot_general(
        g_pre, weight_in, (((1,), (1,)), ((), ())), preferred_element_type=jnp.float32
    )
    g_message = ((g_normed - unit * jnp.mean(g_normed * unit, -1, keepdims=True)) / scale).astype(
        jnp.bfloat16
    )
    chan_update, chan_gradient = (
        lax.all_to_all(update, "chan", split_axis=1, concat_axis=0, tiled=True),
        lax.all_to_all(g_message, "chan", split_axis=1, concat_axis=0, tiled=True),
    )
    output = (features.astype(jnp.float32) + chan_update.astype(jnp.float32)).astype(jnp.bfloat16)
    feature_grad = ewald(False, n, total_rows, phases, chan_gradient, filt, cotangent)
    return (output, feature_grad)


def solution(mesh):
    placed = (
        P("atoms", "chan"),
        P(None, "atoms"),
        P(),
        P(None, "chan"),
        P(),
        P(),
        P("atoms", "chan"),
    )
    return jax.shard_map(
        shards,
        mesh=mesh,
        in_specs=placed,
        out_specs=(P("atoms", "chan"), P("atoms", "chan")),
        check_vma=False,
    )
```

time: 308 us -> 141 us (0.46)
  waiting for transfers between devices: 138 us -> 24.4 us
  Pallas kernels: 0 us -> 70.1 us
  other arithmetic: 76.1 us -> 7.8 us
  matrix products: 53.3 us -> 11 us
  between operations: 14.2 us -> 0.86 us
    psum x2 -> x0, waiting for transfers between devices: 112 us -> none  [ewald(): totals = lax.psum(partial_value, 'atoms')]
    another operation x1, other arithmetic: 72.1 us -> 0.83 us
    pallas_call x0 -> x2, Pallas kernels: none -> 70.1 us  [ewald(): pl.pallas_call(functools.partial(ewald_kernel, first, n, chunks), out_sha...]
    dot_general x5 -> x1, matrix products: 43.1 us -> 0.67 us  [own_filter(): jnp.dot(basis, radial_weight, precision=lax.Precision.HIGHEST, preferred_...]
    all_to_all x1, waiting for transfers between devices: 3.85 us -> 0.01 us  [shards(): lax.all_to_all(update, 'chan', split_axis=1, concat_axis=0, tiled=True)]
  transfers between devices with their start and end apart: 6 -> 4, of which waited for: 5 -> 2; matrix products, arithmetic and copies ran while one was open for 9% -> 6% of each run, Pallas kernels for 0% -> 50%
where the time goes in v1:
time: 141 us; the launch traced here: 140 us
  Pallas kernels  70.1 us (50%)
  waiting for transfers between devices  24.4 us (17%)
  starting transfers between devices  19.1 us (14%)
  matrix products  11 us (8%)
  other arithmetic  7.8 us (6%)
  local copies, waits for them, and re-layouts  7.08 us (5%)
    pallas_call x2, Pallas kernels, ewald(): pl.pallas_call(functools.partial(ewald_kernel, first, n, chunks), out_sha...  70.1 us
    all_to_all x1, waiting for transfers between devices, shards(): lax.all_to_all(message, 'chan', split_axis=0, concat_axis=1, tiled=True)  14 us
    all_to_all x1, waiting for transfers between devices, shards(): lax.all_to_all(g_message, 'chan', split_axis=1, concat_axis=0, tiled=True)  10.5 us
    all_to_all x1, starting transfers between devices, shards(): lax.all_to_all(cotangent, 'chan', split_axis=0, concat_axis=1, tiled=True)  6.46 us
    all_to_all x1, starting transfers between devices, shards(): lax.all_to_all(message, 'chan', split_axis=0, concat_axis=1, tiled=True)  4.89 us
    dot_general x1, matrix products, shards(): lax.dot_general(g_pre, weight_in, (((1,), (1,)), ((), ())), preferred_ele...  4.64 us
    all_to_all x1, starting transfers between devices, shards(): lax.all_to_all(update, 'chan', split_axis=1, concat_axis=0, tiled=True)  4.33 us
    dot_general x1, matrix products, shards(): jnp.dot(hidden, weight_out, preferred_element_type=jnp.float32)  3.6 us
  transfers between devices with their start and end apart: 4, of which 2 were waited for; matrix products, arithmetic and copies ran while one was open for 6% of the time, Pallas kernels for 50%

profile of v1, /device:TPU:0, one launch (start us, length us, event | category | flops | bytes accessed | tf_op | source)
XLA Modules:
  0.0 140.4 jit_solution(12641858717164229086)
XLA Ops:
  0.6 0.0 copy-start
  0.6 0.0 copy-start.4
  0.7 0.0 copy-start.2
  0.7 6.5 %all-to-all-start.2 = ((bf16[4,512,128]{2,1,0:T(8,128)(2,1)}), bf16[4,512,128]{2,1,0:T(8,128)(2,1)S(1)}, u32[]{:S(2)}, u32[]{:S(2)}) async-start(bf16[4,512,128]{2,1,0:T(8,128)(2,1)} %bitcast.33), calls=%async_computation.2 | async-start | bytes 1048576 | tf_op jit(solution)/shard_map/all_to_all | solution.py:268
  7.1 0.8 reshape.52
  7.9 0.8 fusion.17
  8.7 0.8 fusion.9
  9.6 0.3 copy.36
  9.9 0.1 pad.10.refs_0_
  10.1 0.0 copy-done.4
  10.1 0.7 convolution_multiply_fusion.refs_3_.refs_2_
  10.8 0.0 copy-done.2
  10.8 39.0 %ewald_first.1 = (bf16[2048,128]{1,0:T(8,128)(2,1)}, bf16[4096,2048]{1,0:T(8,128)(2,1)}) custom-call(bf16[2048,16]{1,0:T(8,128)(2,1)S(1)} %pad.10.refs_0_, bf16[16,2048]{1,0:T(8,128)(2,1)S(1)} %fusion.8.refs_1_, bf16[2048,128]{1,0:T(8,128)(2,1)S(1)} %copy-done.2, f32[512,128]{1,0:T(8,128)S(1)} %convolution_multiply_fusion.refs_3_.refs_2_), custom_call_target="tpu_custom_call" | custom-call | tf_op jit(solution)/shard_map/ewald_first/pallas_call | solution.py:215
  49.8 0.0 all-to-all-done.2
  49.8 4.9 %all-to-all-start = ((bf16[4,512,128]{2,1,0:T(8,128)(2,1)}), bf16[4,512,128]{2,1,0:T(8,128)(2,1)S(1)}, u32[]{:S(2)}, u32[]{:S(2)}) async-start(bf16[4,512,128]{2,1,0:T(8,128)(2,1)} %bitcast.3), calls=%async_computation | async-start | bytes 1048576 | tf_op jit(solution)/shard_map/all_to_all | solution.py:267
  54.7 1.0 copy.39
  55.7 14.0 %all-to-all-done = bf16[4,512,128]{2,1,0:T(8,128)(2,1)S(1)} async-done(((bf16[4,512,128]{2,1,0:T(8,128)(2,1)}), bf16[4,512,128]{2,1,0:T(8,128)(2,1)S(1)}, u32[]{:S(2)}, u32[]{:S(2)}) %all-to-all-start) | async-done | bytes 524320 | tf_op jit(solution)/shard_map/all_to_all | solution.py:267
  69.6 0.2 fusion.1
  69.8 0.1 convert_bitcast_fusion
  69.9 0.3 copy.37
  70.3 0.1 bitcast_divide_fusion
  70.4 0.0 copy-done
  70.4 2.1 %fusion.4 = f32[512,1024]{1,0:T(8,128)} fusion(bf16[512,1024]{1,0:T(8,128)(2,1)S(1)} %copy-done, f32[512,512]{0,1:T(8,128)S(1)} %bitcast_divide_fusion), kind=kOutput, calls=%fused_computation.16 | convolution fusion | flops 537133056 | bytes 4194304 | tf_op jit(solution)/shard_map/dot_general | solution.py:274
  72.5 4.6 %multiply_reduce_fusion = (f32[512]{0:T(512)S(1)}, f32[512,512]{0,1:T(8,128)}) fusion(f32[512,512]{0,1:T(8,128)S(1)} %bitcast_divide_fusion, bf16[512,1024]{1,0:T(8,128)(2,1)S(1)} %copy-done, f32[512,1024]{1,0:T(8,128)} %fusion.4, bf16[512,512]{0,1:T(8,128)(2,1)} %bitcast.37, bf16[1024,512]{1,0:T(8,128)(2,1)} %param.12), kind=kOutput, calls=%fused_computation.14 | convolution fusion | flops 1078984192 | bytes 6817792 | tf_op jit(solution)/shard_map/dot_general | solution.py:282
  77.1 1.4 divide_convert_fusion
  78.5 1.0 copy.40
  79.5 3.5 %all-to-all-start.3 = ((bf16[512,4,128]{2,0,1:T(8,128)(2,1)}), bf16[512,4,128]{2,0,1:T(8,128)(2,1)S(1)}, u32[]{:S(2)}, u32[]{:S(2)}) async-start(bf16[512,4,128]{2,0,1:T(8,128)(2,1)} %copy.40), calls=%async_computation.3 | async-start | bytes 1048576 | tf_op jit(solution)/shard_map/all_to_all | solution.py:290
  83.0 0.0 copy-start.1
  83.0 3.6 %convolution_convert_fusion = bf16[512,512]{0,1:T(8,128)(2,1)} fusion(bf16[1024,512]{1,0:T(8,128)(2,1)} %param.12, f32[512,1024]{1,0:T(8,128)} %fusion.4), kind=kOutput, calls=%fused_computation.5 | convolution fusion | flops 539754496 | bytes 3670016 | tf_op jit(solution)/shard_map/dot_general | solution.py:276
  86.6 10.5 %all-to-all-done.3 = bf16[512,4,128]{2,0,1:T(8,128)(2,1)S(1)} async-done(((bf16[512,4,128]{2,0,1:T(8,128)(2,1)}), bf16[512,4,128]{2,0,1:T(8,128)(2,1)S(1)}, u32[]{:S(2)}, u32[]{:S(2)}) %all-to-all-start.3) | async-done | bytes 524320 | tf_op jit(solution)/shard_map/all_to_all | solution.py:290
  97.1 4.3 %all-to-all-start.1 = ((bf16[512,4,128]{0,2,1:T(8,128)(2,1)}), bf16[512,4,128]{0,2,1:T(8,128)(2,1)}, u32[]{:S(2)}, u32[]{:S(2)}) async-start(bf16[512,4,128]{0,2,1:T(8,128)(2,1)} %bitcast.6), calls=%async_computation.1 | async-start | bytes 1048576 | tf_op jit(solution)/shard_map/all_to_all | solution.py:289
  101.4 0.0 copy-done.1
  101.4 31.1 %ewald_second.1 = f32[2048,128]{1,0:T(8,128)S(1)} custom-call(bf16[4096,2048]{1,0:T(8,128)(2,1)} %get-tuple-element.5.refs_0_, bf16[2048,128]{1,0:T(8,128)(2,1)S(1)} %bitcast.34, f32[512,128]{1,0:T(8,128)S(1)} %convolution_multiply_fusion.refs_3_.refs_2_, bf16[2048,128]{1,0:T(8,128)(2,1)S(1)} %copy-done.1), custom_call_target="tpu_custom_call" | custom-call | tf_op jit(solution)/shard_map/ewald_second/pallas_call | solution.py:215
  132.6 0.0 copy-start.3
  132.6 0.0 all-to-all-done.1
  132.6 2.2 %convert_bitcast_fusion.1 = f32[4,512,128]{1,2,0:T(8,128)} fusion(bf16[512,4,128]{0,2,1:T(8,128)(2,1)} %all-to-all-done.1), kind=kLoop, calls=%fused_computation.12 | loop fusion | flops 262144 | bytes 1572864 | tf_op jit(solution)/shard_map/convert_element_type | solution.py:292
  134.8 2.5 %copy.38 = f32[4,512,128]{2,1,0:T(8,128)} copy(f32[4,512,128]{1,2,0:T(8,128)} %convert_bitcast_fusion.1) | data formatting | bytes 2097152 | tf_op jit(solution)/shard_map/convert_element_type | solution.py:292
  137.3 0.0 copy-done.3
  137.3 2.1 %fusion.2 = bf16[2048,128]{1,0:T(8,128)(2,1)} fusion(f32[4,512,128]{2,1,0:T(8,128)} %copy.38, bf16[2048,128]{1,0:T(8,128)(2,1)S(1)} %copy-done.3), kind=kLoop, calls=%fused_computation.10 | loop fusion | flops 786432 | bytes 2097152 | tf_op jit(solution)/shard_map/convert_element_type | solution.py:292
  139.5 1.0 copy.42
  (7 shorter events, 0.1 us)
Async XLA Ops:
  0.6 69.8 %copy-start = (bf16[512,1024]{1,0:T(8,128)(2,1)S(1)}, bf16[512,1024]{1,0:T(8,128)(2,1)}, u32[]{:S(2)}) copy-start(bf16[512,1024]{1,0:T(8,128)(2,1)} %param.11) | copy-start | bytes 3145732
  0.6 9.4 %copy-start.4 = (f32[16,128]{1,0:T(8,128)S(1)}, f32[16,128]{1,0:T(8,128)}, u32[]{:S(2)}) copy-start(f32[16,128]{1,0:T(8,128)} %param.10) | copy-start | bytes 24580
  0.7 10.1 %copy-start.2 = (bf16[2048,128]{1,0:T(8,128)(2,1)S(1)}, bf16[2048,128]{1,0:T(8,128)(2,1)}, u32[]{:S(2)}) copy-start(bf16[2048,128]{1,0:T(8,128)(2,1)} %refs_2_.1) | copy-start | bytes 1572868
  0.7 49.1 %all-to-all-start.2 = ((bf16[4,512,128]{2,1,0:T(8,128)(2,1)}), bf16[4,512,128]{2,1,0:T(8,128)(2,1)S(1)}, u32[]{:S(2)}, u32[]{:S(2)}) async-start(bf16[4,512,128]{2,1,0:T(8,128)(2,1)} %bitcast.33), calls=%async_computation.2 | async-start | bytes 1048576 | tf_op jit(solution)/shard_map/all_to_all | solution.py:268
  49.8 19.9 %all-to-all-start = ((bf16[4,512,128]{2,1,0:T(8,128)(2,1)}), bf16[4,512,128]{2,1,0:T(8,128)(2,1)S(1)}, u32[]{:S(2)}, u32[]{:S(2)}) async-start(bf16[4,512,128]{2,1,0:T(8,128)(2,1)} %bitcast.3), calls=%async_computation | async-start | bytes 1048576 | tf_op jit(solution)/shard_map/all_to_all | solution.py:267
  79.5 17.6 %all-to-all-start.3 = ((bf16[512,4,128]{2,0,1:T(8,128)(2,1)}), bf16[512,4,128]{2,0,1:T(8,128)(2,1)S(1)}, u32[]{:S(2)}, u32[]{:S(2)}) async-start(bf16[512,4,128]{2,0,1:T(8,128)(2,1)} %copy.40), calls=%async_computation.3 | async-start | bytes 1048576 | tf_op jit(solution)/shard_map/all_to_all | solution.py:290
  83.0 18.4 %copy-start.1 = (bf16[2048,128]{1,0:T(8,128)(2,1)S(1)}, bf16[2048,128]{1,0:T(8,128)(2,1)}, u32[]{:S(2)}) copy-start(bf16[2048,128]{1,0:T(8,128)(2,1)} %refs_3_.1) | copy-start | bytes 1572868
  97.1 35.5 %all-to-all-start.1 = ((bf16[512,4,128]{0,2,1:T(8,128)(2,1)}), bf16[512,4,128]{0,2,1:T(8,128)(2,1)}, u32[]{:S(2)}, u32[]{:S(2)}) async-start(bf16[512,4,128]{0,2,1:T(8,128)(2,1)} %bitcast.6), calls=%async_computation.1 | async-start | bytes 1048576 | tf_op jit(solution)/shard_map/all_to_all | solution.py:289
  132.6 4.8 %copy-start.3 = (bf16[2048,128]{1,0:T(8,128)(2,1)S(1)}, bf16[2048,128]{1,0:T(8,128)(2,1)}, u32[]{:S(2)}) copy-start(bf16[2048,128]{1,0:T(8,128)(2,1)} %refs_2_.1) | copy-start | bytes 1572868

commit v2 on v1

v2 whole, which is shorter than its diff:
```python
import functools
import math

import jax
import jax.numpy as jnp
import numpy as np
from jax import lax
from jax.experimental import pallas as pl
from jax.experimental.pallas import tpu as pltpu
from jax.sharding import PartitionSpec as P

NB = 16
KMAX = 8
GRID = 4096
MESH = pl.DeviceIdType.MESH
BLOCK = 128


def fit_even(fn, degree):
    cheb = np.polynomial.chebyshev.Chebyshev.interpolate(
        lambda u: fn(np.sqrt(u)), degree, domain=[0.0, 0.25]
    )
    return [float(v) for v in cheb.convert(kind=np.polynomial.Polynomial, domain=[-1, 1], window=[-1, 1]).coef]


def sin_over(f):
    return math.sqrt(2.0) * math.pi * np.sinc(f)


def cos_half(f):
    return math.sqrt(2.0) * np.cos(math.pi * f)


SIN_COEF = fit_even(sin_over, 3)
COS_COEF = fit_even(cos_half, 3)


def horner(coef, u):
    total = coef[-1] * u + coef[-2]
    for c in coef[-3::-1]:
        total = total * u + c
    return total


def layer_kernel(n, nc, chunks, *refs):
    (waves_in, place_in, x_ref, filt_ref, w_in, w_out, cot_ref, out_ref, grad_ref,
     wave_ref, place_ref, ph, part, rs_src, rs_dst, ag, acc,
     cot_rx, msg_tx, msg_rx, upd_tx, upd_rx, grd_tx, grd_rx,
     rs_send, rs_recv, ag_send, ag_recv, cot_send, cot_recv,
     msg_send, msg_recv, upd_send, upd_recv, grd_send, grd_recv) = refs
    me = lax.axis_index("atoms")
    mc = lax.axis_index("chan")
    atoms, channels = x_ref.shape
    rows = n * BLOCK
    waves = rows // 2
    own = atoms // nc
    sub = min(BLOCK, own)
    subs = own // sub
    f32, bf16 = jnp.float32, jnp.bfloat16

    def peers(fn):
        def body(step, carry):
            fn(lax.rem(me + step, n))
            return carry

        lax.fori_loop(1, n, body, 0)

    def chan_peers(fn):
        def body(step, carry):
            fn(lax.rem(mc + step, nc))
            return carry

        lax.fori_loop(1, nc, body, 0)

    barrier = pltpu.get_barrier_semaphore()
    peers(lambda peer: pl.semaphore_signal(
        barrier, inc=1, device_id={"atoms": peer}, device_id_type=MESH))
    chan_peers(lambda peer: pl.semaphore_signal(
        barrier, inc=1, device_id={"chan": peer}, device_id_type=MESH))

    def rs_copy(j, here, there):
        return pltpu.make_async_remote_copy(
            src_ref=rs_src.at[j, there],
            dst_ref=rs_dst.at[j, here],
            send_sem=rs_send.at[j, there],
            recv_sem=rs_recv.at[j, here],
            device_id={"atoms": there},
            device_id_type=MESH,
        )

    def ag_copy(j, owner, there):
        return pltpu.make_async_remote_copy(
            src_ref=ag.at[j, owner],
            dst_ref=ag.at[j, owner],
            send_sem=ag_send.at[j, there],
            recv_sem=ag_recv.at[j, owner],
            device_id={"atoms": there},
            device_id_type=MESH,
        )

    def cot_copy(here, there):
        return pltpu.make_async_remote_copy(
            src_ref=cot_ref.at[pl.ds(pl.multiple_of(there * own, own), own)],
            dst_ref=cot_rx.at[here],
            send_sem=cot_send.at[there],
            recv_sem=cot_recv.at[here],
            device_id={"chan": there},
            device_id_type=MESH,
        )

    def sub_copy(src, dst, send, recv, t, here, there):
        span = pl.ds(t * sub, sub)
        return pltpu.make_async_remote_copy(
            src_ref=src.at[there, span],
            dst_ref=dst.at[here, span],
            send_sem=send.at[t, there],
            recv_sem=recv.at[t, here],
            device_id={"chan": there},
            device_id_type=MESH,
        )

    msg_copy = functools.partial(sub_copy, msg_tx, msg_rx, msg_send, msg_recv)
    upd_copy = functools.partial(sub_copy, upd_tx, upd_rx, upd_send, upd_recv)
    grd_copy = functools.partial(sub_copy, grd_tx, grd_rx, grd_send, grd_recv)

    k = waves_in[...].astype(f32)
    wave_ref[...] = jnp.concatenate(
        [k * (64.0 / GRID), k * (1.0 / GRID), jnp.zeros((10, k.shape[1]), f32)], 0
    ).astype(bf16)
    r = place_in[...]
    high = lax.shift_right_logical(r, 6)
    place_ref[...] = jnp.concatenate(
        [high.astype(f32), (r - high * 64).astype(f32), jnp.zeros((10, r.shape[1]), f32)], 0
    ).astype(bf16)

    tile = min(256, atoms)

    def generate(j):
        top = j * rows

        def body(a, carry):
            cols = pl.ds(pl.multiple_of(a * tile, tile), tile)
            turns = lax.dot_general(
                wave_ref[:, pl.ds(j * waves, waves)], place_ref[:, cols],
                (((0,), (0,)), ((), ())), preferred_element_type=f32,
            )
            f = turns - jnp.round(turns)
            u = f * f
            s = f * horner(SIN_COEF, u)
            c = horner(COS_COEF, u)
            ph[pl.ds(top, waves), cols] = (1.0 - s * s).astype(bf16)
            ph[pl.ds(top + waves, waves), cols] = (s * c).astype(bf16)
            return carry

        lax.fori_loop(0, atoms // tile, body, 0)

    group = min(4, n)

    def project(j, field):
        def body(i, carry):
            span = pl.ds(pl.multiple_of(j * rows + i * (group * BLOCK), group * BLOCK), group * BLOCK)
            value = jnp.dot(ph[span, :], field(), preferred_element_type=f32)
            value = value.reshape(group, BLOCK, value.shape[-1])
            slots = pl.ds(i * group, group)
            part[j, slots] = value
            rs_src[j, slots] = value.astype(bf16)
            return carry

        lax.fori_loop(0, n // group, body, 0)

    def reduce(j):
        part_own = part[j, me]

        def body(step, total):
            peer = lax.rem(me + step, n)
            rs_copy(j, peer, me).wait_recv()
            return total + rs_dst[j, peer].astype(f32)

        total = lax.fori_loop(1, n, body, part_own)
        shaped = filt_ref[pl.ds(j * BLOCK, BLOCK), :] * total
        ag[j, me] = shaped.T.astype(bf16)
        peers(lambda peer: ag_copy(j, me, peer).start())

    def back(j, emit):
        peers(lambda peer: ag_copy(j, peer, me).wait_recv())
        lhs = jnp.concatenate([ag[j, d] for d in range(n)], axis=1)

        def body(a, carry):
            cols = pl.ds(pl.multiple_of(a * own, own), own)
            value = jnp.dot(lhs, ph[pl.ds(j * rows, rows), cols], preferred_element_type=f32)
            if j > 0:
                value = value + acc[:, cols]
            if j < chunks - 1:
                acc[:, cols] = value
            else:
                emit(a, value.T)
            return carry

        lax.fori_loop(0, nc, body, 0)

    def ewald(first, field, emit):
        for j in range(chunks + 2):
            if j < chunks:
                if first:
                    generate(j)
                project(j, field)
                if first and j == 0:
                    pl.semaphore_wait(barrier, n - 1 + nc - 1)
                    chan_peers(lambda peer: cot_copy(mc, peer).start())
                peers(lambda peer: rs_copy(j, me, peer).start())
            if 1 <= j <= chunks:
                reduce(j - 1)
            if j >= 2:
                back(j - 2, emit)
        for j in range(chunks):
            peers(lambda peer: rs_copy(j, me, peer).wait_send())
            peers(lambda peer: ag_copy(j, me, peer).wait_send())

    def emit_message(a, value):
        msg_tx[a] = value.astype(bf16)

    ewald(True, lambda: x_ref[...], emit_message)

    for t in range(subs):
        chan_peers(lambda peer: msg_copy(t, mc, peer).start())
    msg_rx[mc] = msg_tx[mc]
    cot_rx[mc] = cot_ref[pl.ds(pl.multiple_of(mc * own, own), own), :]
    chan_peers(lambda peer: cot_copy(peer, mc).wait_recv())

    for t in range(subs):
        span = pl.ds(t * sub, sub)
        chan_peers(lambda peer: msg_copy(t, peer, mc).wait_recv())
        message = jnp.concatenate([msg_rx[c, span, :] for c in range(nc)], 1).astype(f32)
        inverse = 1.0 / jnp.sqrt(jnp.mean(message * message, -1, keepdims=True) + 1e-06)
        unit = message * inverse
        pre = jnp.dot(unit.astype(bf16), w_in[...], preferred_element_type=f32)
        gate = jax.nn.sigmoid(pre)
        update = jnp.dot((pre * gate).astype(bf16), w_out[...], preferred_element_type=f32)
        cot = jnp.concatenate([cot_rx[c, span, :] for c in range(nc)], 1)
        g_hidden = lax.dot_general(
            cot, w_out[...], (((1,), (1,)), ((), ())), preferred_element_type=f32
        )
        g_pre = (g_hidden * gate * (1.0 + pre * (1.0 - gate))).astype(bf16)
        g_normed = lax.dot_general(
            g_pre, w_in[...], (((1,), (1,)), ((), ())), preferred_element_type=f32
        )
        g_message = (
            (g_normed - unit * jnp.mean(g_normed * unit, -1, keepdims=True)) * inverse
        ).astype(bf16)
        update = update.astype(bf16)
        for c in range(nc):
            grd_tx[c, span, :] = g_message[:, c * channels:(c + 1) * channels]
            upd_tx[c, span, :] = update[:, c * channels:(c + 1) * channels]
        chan_peers(lambda peer: grd_copy(t, mc, peer).start())

    for t in range(subs):
        chan_peers(lambda peer: upd_copy(t, mc, peer).start())
    grd_rx[mc] = grd_tx[mc]
    upd_rx[mc] = upd_tx[mc]
    for t in range(subs):
        chan_peers(lambda peer: grd_copy(t, peer, mc).wait_recv())

    def emit_grad(a, value):
        span = pl.ds(pl.multiple_of(a * own, own), own)
        grad_ref[span, :] = cot_ref[span, :].astype(f32) + value

    ewald(False, lambda: grd_rx[...].reshape(atoms, channels), emit_grad)

    for t in range(subs):
        chan_peers(lambda peer: upd_copy(t, peer, mc).wait_recv())

    def add_update(c, carry):
        span = pl.ds(pl.multiple_of(c * own, own), own)
        out_ref[span, :] = (x_ref[span, :].astype(f32) + upd_rx[c].astype(f32)).astype(bf16)
        return carry

    lax.fori_loop(0, nc, add_update, 0)
    chan_peers(lambda peer: cot_copy(mc, peer).wait_send())
    for t in range(subs):
        chan_peers(lambda peer: msg_copy(t, mc, peer).wait_send())
        chan_peers(lambda peer: grd_copy(t, mc, peer).wait_send())
        chan_peers(lambda peer: upd_copy(t, mc, peer).wait_send())


def layer(n, nc, wavevectors, positions, features, filt, weight_in, weight_out, cotangent):
    atoms, channels = features.shape
    total_rows = 2 * wavevectors.shape[1]
    chunks = total_rows // (n * BLOCK)
    own = atoms // nc
    subs = own // min(BLOCK, own)
    vmem = pl.BlockSpec(memory_space=pltpu.VMEM)
    block = (chunks, n, BLOCK, channels)
    spread = pltpu.VMEM((nc, own, channels), jnp.bfloat16)
    atom_sems = pltpu.SemaphoreType.DMA((chunks, n))
    one_sem = pltpu.SemaphoreType.DMA((nc,))
    sub_sems = pltpu.SemaphoreType.DMA((subs, nc))
    return pl.pallas_call(
        functools.partial(layer_kernel, n, nc, chunks),
        out_shape=(
            jax.ShapeDtypeStruct((atoms, channels), jnp.bfloat16),
            jax.ShapeDtypeStruct((atoms, channels), jnp.float32),
        ),
        in_specs=[vmem] * 7,
        out_specs=(vmem, vmem),
        scratch_shapes=[
            pltpu.VMEM((16, wavevectors.shape[1]), jnp.bfloat16),
            pltpu.VMEM((16, atoms), jnp.bfloat16),
            pltpu.VMEM((total_rows, atoms), jnp.bfloat16),
            pltpu.VMEM(block, jnp.float32),
            pltpu.VMEM(block, jnp.bfloat16),
            pltpu.VMEM(block, jnp.bfloat16),
            pltpu.VMEM((chunks, n, channels, BLOCK), jnp.bfloat16),
            pltpu.VMEM((channels, atoms), jnp.float32),
        ] + [spread] * 7 + [atom_sems] * 4 + [one_sem] * 2 + [sub_sems] * 6,
        compiler_params=pltpu.CompilerParams(
            collective_id=0, has_side_effects=True, vmem_limit_bytes=48 * 2**20
        ),
        name="layer",
    )(wavevectors, positions, features, filt, weight_in, weight_out, cotangent)


def own_filter(wavevectors, radial_weight, atom_count, n, me):
    kvec = wavevectors.shape[1]
    waves = n * BLOCK // 2
    chunked = wavevectors.reshape(3, kvec // waves, n // 2, BLOCK)
    own = lax.dynamic_index_in_dim(chunked, lax.rem(me, n // 2), 2, keepdims=False).reshape(3, -1)
    lengths = jnp.sqrt(jnp.sum((own * own).astype(jnp.float32), 0))
    spacing = KMAX * math.sqrt(3.0) / (NB - 1)
    centers = jnp.arange(NB).astype(jnp.float32) * spacing
    basis = jnp.exp(-0.5 * ((lengths[:, None] - centers[None, :]) / spacing) ** 2)
    filt = jnp.dot(
        basis, radial_weight, precision=lax.Precision.HIGHEST, preferred_element_type=jnp.float32
    )
    return filt * (2.0 * kvec * atom_count) ** (-0.5)


def shards(features, positions, wavevectors, radial_weight, weight_in, weight_out, cotangent):
    local_atoms = features.shape[0]
    n = lax.axis_size("atoms")
    atom_count = local_atoms * n
    filt = own_filter(wavevectors, radial_weight, atom_count, n, lax.axis_index("atoms"))
    return layer(
        n, lax.axis_size("chan"), wavevectors, positions, features, filt,
        weight_in, weight_out, cotangent,
    )


def solution(mesh):
    placed = (
        P("atoms", "chan"),
        P(None, "atoms"),
        P(),
        P(None, "chan"),
        P(),
        P(),
        P("atoms", "chan"),
    )
    return jax.shard_map(
        shards,
        mesh=mesh,
        in_specs=placed,
        out_specs=(P("atoms", "chan"), P("atoms", "chan")),
        check_vma=False,
    )
```

time: 141 us -> 109 us (0.77); the launches traced: 140 us -> 107 us
  Pallas kernels: 70.1 us -> 98.4 us
  waiting for transfers between devices: 24.4 us -> 0 us
  starting transfers between devices: 19.1 us -> 0 us
  matrix products: 11 us -> 0.67 us
  other arithmetic: 7.8 us -> 0.04 us
    pallas_call x2 -> x1, Pallas kernels: 70.1 us -> 98.4 us  [layer(): pl.pallas_call(functools.partial(layer_kernel, n, nc, chunks), out_shape=...]
    all_to_all x4 -> x0, waiting for transfers between devices: 24.4 us -> none  [the longest x1 14 us: shards(): lax.all_to_all(message, 'chan', split_axis=0, concat_axis=1, tiled=True)]
    all_to_all x4 -> x0, starting transfers between devices: 19.1 us -> none  [the longest x1 6.46 us: shards(): lax.all_to_all(cotangent, 'chan', split_axis=0, concat_axis=1, tiled=True)]
    dot_general x3 -> x0, matrix products: 10.3 us -> none  [the longest x1 4.64 us: shards(): lax.dot_general(g_pre, weight_in, (((1,), (1,)), ((), ())), preferred_ele...]
    convert_element_type x4 -> x0, other arithmetic: 5.79 us -> none  [the longest x1 2.2 us: shards(): chan_update.astype(jnp.float32)]
    unnamed x11 -> x16, local copies, waits for them, and re-layouts: 1 us -> 6.39 us
    convert_element_type x2 -> x0, local copies, waits for them, and re-layouts: 2.86 us -> none  [the longest x1 2.53 us: shards(): chan_update.astype(jnp.float32)]
    all_to_all x2 -> x0, local copies, waits for them, and re-layouts: 2.01 us -> none  [the longest x1 1.01 us: shards(): lax.all_to_all(cotangent, 'chan', split_axis=0, concat_axis=1, tiled=True)]
  transfers between devices with their start and end apart: 4 -> 0, of which waited for: 2 -> 0; matrix products, arithmetic and copies ran while one was open for 6% -> 0% of each run, Pallas kernels for 50% -> 0%
where the time goes in v2:
time: 109 us; the launch traced here: 107 us
  Pallas kernels  98.4 us (90%)
  local copies, waits for them, and re-layouts  7.18 us (7%)
    pallas_call x1, Pallas kernels, layer(): pl.pallas_call(functools.partial(layer_kernel, n, nc, chunks), out_shape=...  98.4 us
    unnamed x16, local copies, waits for them, and re-layouts  6.39 us

profile of v2, /device:TPU:0, one launch (start us, length us, event | category | flops | bytes accessed | tf_op | source)
XLA Modules:
  0.0 107.0 jit_solution(4887417704987571483)
XLA Ops:
  0.6 0.0 copy-start
  0.7 0.8 reshape.24
  1.5 0.0 copy-done
  1.5 0.0 copy-start.5
  1.5 0.0 copy-start.6
  1.5 0.7 convolution_multiply_fusion.refs_3_
  2.2 0.1 copy-done.5
  2.3 0.0 copy-done.6
  2.3 0.0 copy-start.1
  2.3 1.2 %copy-done.1 = bf16[512,1024]{1,0:T(8,128)(2,1)S(1)} copy-done((bf16[512,1024]{1,0:T(8,128)(2,1)S(1)}, bf16[512,1024]{1,0:T(8,128)(2,1)}, u32[]{:S(2)}) %copy-start.1) | copy-done | bytes 1048600
  3.5 0.0 copy-start.2
  3.5 1.2 %copy-done.2 = bf16[1024,512]{1,0:T(8,128)(2,1)S(1)} copy-done((bf16[1024,512]{1,0:T(8,128)(2,1)S(1)}, bf16[1024,512]{1,0:T(8,128)(2,1)}, u32[]{:S(2)}) %copy-start.2) | copy-done | bytes 1048600
  4.7 0.0 copy-start.3
  4.7 1.0 copy-done.3
  5.8 0.0 copy-start.4
  5.8 1.0 copy-done.4
  6.8 98.4 %layer.1 = (bf16[2048,128]{1,0:T(8,128)(2,1)S(1)}, f32[2048,128]{1,0:T(8,128)S(1)}) custom-call(s32[3,2048]{1,0:T(4,128)S(1)} %copy-done.5, s32[3,2048]{1,0:T(4,128)S(1)} %copy-done.6, bf16[2048,128]{1,0:T(8,128)(2,1)S(1)} %copy-done.3, f32[512,128]{1,0:T(8,128)S(1)} %convolution_multiply_fusion.refs_3_, bf16[512,1024]{1,0:T(8,128)(2,1)S(1)} %copy-done.1, ...), custom_call_target="tpu_custom_call" | custom-call | tf_op jit(solution)/shard_map/layer/pallas_call | solution.py:297
  105.2 0.8 copy.11
  106.0 1.0 copy.12
  (3 shorter events, 0.0 us)
Async XLA Ops:
  0.6 0.9 copy-start
  1.5 0.8 copy-start.5
  1.5 0.8 copy-start.6
  2.3 1.2 %copy-start.1 = (bf16[512,1024]{1,0:T(8,128)(2,1)S(1)}, bf16[512,1024]{1,0:T(8,128)(2,1)}, u32[]{:S(2)}) copy-start(bf16[512,1024]{1,0:T(8,128)(2,1)} %refs_4_.1) | copy-start | bytes 3145732
  3.5 1.2 %copy-start.2 = (bf16[1024,512]{1,0:T(8,128)(2,1)S(1)}, bf16[1024,512]{1,0:T(8,128)(2,1)}, u32[]{:S(2)}) copy-start(bf16[1024,512]{1,0:T(8,128)(2,1)} %refs_5_.1) | copy-start | bytes 3145732
  4.7 1.0 copy-start.3
  5.8 1.0 copy-start.4

commit v3 on v2

--- a/solution.py
+++ b/solution.py
@@ -43,11 +43,20 @@
 
 
 def layer_kernel(n, nc, chunks, *refs):
-    (waves_in, place_in, x_ref, filt_ref, w_in, w_out, cot_ref, out_ref, grad_ref,
-     wave_ref, place_ref, ph, part, rs_src, rs_dst, ag, acc,
+    (waves_in, place_in, x_hbm, filt_ref, w_in_hbm, w_out_hbm, cot_hbm, out_ref, grad_ref,
+     x_ref, cot_ref, w_in, w_out, fetch_sem,
+     wave_ref, place_ref, ph, part, pair_tx, pair_rx, hop_tx, hop_rx, ag, acc,
      cot_rx, msg_tx, msg_rx, upd_tx, upd_rx, grd_tx, grd_rx,
-     rs_send, rs_recv, ag_send, ag_recv, cot_send, cot_recv,
+     pair_send, pair_recv, fwd_send, fwd_recv, hop_send, hop_recv, ag_send, ag_recv, cot_send, cot_recv,
      msg_send, msg_recv, upd_send, upd_recv, grd_send, grd_recv) = refs
+    fetch = [
+        pltpu.make_async_copy(src, dst, fetch_sem.at[i])
+        for i, (src, dst) in enumerate(
+            ((x_hbm, x_ref), (cot_hbm, cot_ref), (w_in_hbm, w_in), (w_out_hbm, w_out))
+        )
+    ]
+    for copy in fetch:
+        copy.start()
     me = lax.axis_index("atoms")
     mc = lax.axis_index("chan")
     atoms, channels = x_ref.shape
@@ -78,25 +87,58 @@
     chan_peers(lambda peer: pl.semaphore_signal(
         barrier, inc=1, device_id={"chan": peer}, device_id_type=MESH))
 
-    def rs_copy(j, here, there):
-        return pltpu.make_async_remote_copy(
-            src_ref=rs_src.at[j, there],
-            dst_ref=rs_dst.at[j, here],
-            send_sem=rs_send.at[j, there],
-            recv_sem=rs_recv.at[j, here],
-            device_id={"atoms": there},
+    half = n // 2
+    chip, core = me // 2, lax.rem(me, 2)
+    mine = core * half
+    sibling = me + 1 - 2 * core
+
+    def pair_copy(j):
+        return pltpu.make_async_remote_copy(
+            src_ref=pair_tx.at[j, pl.ds((1 - core) * half, half)],
+            dst_ref=pair_rx.at[j],
+            send_sem=pair_send.at[j],
+            recv_sem=pair_recv.at[j],
+            device_id={"atoms": sibling},
+            device_id_type=MESH,
+        )
+
+    def hop_copy(j, here, there):
+        return pltpu.make_async_remote_copy(
+            src_ref=hop_tx.at[j, there],
+            dst_ref=hop_rx.at[j, here],
+            send_sem=hop_send.at[j, there],
+            recv_sem=hop_recv.at[j, here],
+            device_id={"atoms": 2 * there + core},
             device_id_type=MESH,
         )
 
     def ag_copy(j, owner, there):
         return pltpu.make_async_remote_copy(
-            src_ref=ag.at[j, owner],
-            dst_ref=ag.at[j, owner],
+            src_ref=ag.at[j, mine + owner],
+            dst_ref=ag.at[j, mine + owner],
             send_sem=ag_send.at[j, there],
             recv_sem=ag_recv.at[j, owner],
-            device_id={"atoms": there},
-            device_id_type=MESH,
-        )
+            device_id={"atoms": 2 * there + core},
+            device_id_type=MESH,
+        )
+
+    def fwd_copy(j, which):
+        span = pl.ds(which * half, half)
+        return pltpu.make_async_remote_copy(
+            src_ref=ag.at[j, span],
+            dst_ref=ag.at[j, span],
+            send_sem=fwd_send.at[j],
+            recv_sem=fwd_recv.at[j],
+            device_id={"atoms": sibling},
+            device_id_type=MESH,
+        )
+
+    def chips(fn):
+        def body(step, carry):
+            fn(lax.rem(chip + step, half))
+            return carry
+
+        lax.fori_loop(1, half, body, 0)
 
     def cot_copy(here, there):
         return pltpu.make_async_remote_copy(
@@ -163,26 +205,39 @@
             value = value.reshape(group, BLOCK, value.shape[-1])
             slots = pl.ds(i * group, group)
             part[j, slots] = value
-            rs_src[j, slots] = value.astype(bf16)
+            pair_tx[j, slots] = value.astype(bf16)
             return carry
 
         lax.fori_loop(0, n // group, body, 0)
 
+    def hop(j):
+        pair_copy(j).wait_recv()
+
+        def send(peer):
+            total = part[j, mine + peer] + pair_rx[j, peer].astype(f32)
+            hop_tx[j, peer] = total.astype(bf16)
+            hop_copy(j, chip, peer).start()
+
+        chips(send)
+
     def reduce(j):
-        part_own = part[j, me]
-
         def body(step, total):
-            peer = lax.rem(me + step, n)
-            rs_copy(j, peer, me).wait_recv()
-            return total + rs_dst[j, peer].astype(f32)
-
-        total = lax.fori_loop(1, n, body, part_own)
+            peer = lax.rem(chip + step, half)
+            hop_copy(j, peer, chip).wait_recv()
+            return total + hop_rx[j, peer].astype(f32)
+
+        start = part[j, mine + chip] + pair_rx[j, chip].astype(f32)
+        total = lax.fori_loop(1, half, body, start)
         shaped = filt_ref[pl.ds(j * BLOCK, BLOCK), :] * total
-        ag[j, me] = shaped.T.astype(bf16)
-        peers(lambda peer: ag_copy(j, me, peer).start())
+        ag[j, mine + chip] = shaped.T.astype(bf16)
+        chips(lambda peer: ag_copy(j, chip, peer).start())
+
+    def forward(j):
+        chips(lambda peer: ag_copy(j, peer, chip).wait_recv())
+        fwd_copy(j, core).start()
 
     def back(j, emit):
-        peers(lambda peer: ag_copy(j, peer, me).wait_recv())
+        fwd_copy(j, 1 - core).wait_recv()
         lhs = jnp.concatenate([ag[j, d] for d in range(n)], axis=1)
 
         def body(a, carry):
@@ -199,22 +254,31 @@
         lax.fori_loop(0, nc, body, 0)
 
     def ewald(first, field, emit):
-        for j in range(chunks + 2):
-            if j < chunks:
+        for i in range(chunks + 4):
+            if i < chunks:
                 if first:
-                    generate(j)
-                project(j, field)
-                if first and j == 0:
+                    generate(i)
+                if first and i == 0:
+                    fetch[0].wait()
+                project(i, field)
+                if first and i == 0:
                     pl.semaphore_wait(barrier, n - 1 + nc - 1)
+                    fetch[1].wait()
                     chan_peers(lambda peer: cot_copy(mc, peer).start())
-                peers(lambda peer: rs_copy(j, me, peer).start())
-            if 1 <= j <= chunks:
-                reduce(j - 1)
-            if j >= 2:
-                back(j - 2, emit)
+                pair_copy(i).start()
+            if 1 <= i <= chunks:
+                hop(i - 1)
+            if 2 <= i <= chunks + 1:
+                reduce(i - 2)
+            if 3 <= i <= chunks + 2:
+                forward(i - 3)
+            if i >= 4:
+                back(i - 4, emit)
         for j in range(chunks):
-            peers(lambda peer: rs_copy(j, me, peer).wait_send())
-            peers(lambda peer: ag_copy(j, me, peer).wait_send())
+            pair_copy(j).wait_send()
+            chips(lambda peer: hop_copy(j, chip, peer).wait_send())
+            chips(lambda peer: ag_copy(j, chip, peer).wait_send())
+            fwd_copy(j, core).wait_send()
 
     def emit_message(a, value):
         msg_tx[a] = value.astype(bf16)
@@ -223,6 +287,8 @@
 
     for t in range(subs):
         chan_peers(lambda peer: msg_copy(t, mc, peer).start())
+    fetch[2].wait()
+    fetch[3].wait()
     msg_rx[mc] = msg_tx[mc]
     cot_rx[mc] = cot_ref[pl.ds(pl.multiple_of(mc * own, own), own), :]
     chan_peers(lambda peer: cot_copy(peer, mc).wait_recv())
@@ -290,8 +356,11 @@
     subs = own // min(BLOCK, own)
     vmem = pl.BlockSpec(memory_space=pltpu.VMEM)
     block = (chunks, n, BLOCK, channels)
+    hbm = pl.BlockSpec(memory_space=pltpu.HBM)
+    halved = pltpu.VMEM((chunks, n // 2, BLOCK, channels), jnp.bfloat16)
     spread = pltpu.VMEM((nc, own, channels), jnp.bfloat16)
-    atom_sems = pltpu.SemaphoreType.DMA((chunks, n))
+    atom_sems = pltpu.SemaphoreType.DMA((chunks, n // 2))
+    chunk_sem = pltpu.SemaphoreType.DMA((chunks,))
     one_sem = pltpu.SemaphoreType.DMA((nc,))
     sub_sems = pltpu.SemaphoreType.DMA((subs, nc))
     return pl.pallas_call(
@@ -300,18 +369,23 @@
             jax.ShapeDtypeStruct((atoms, channels), jnp.bfloat16),
             jax.ShapeDtypeStruct((atoms, channels), jnp.float32),
         ),
-        in_specs=[vmem] * 7,
+        in_specs=[vmem, vmem, hbm, vmem, hbm, hbm, hbm],
         out_specs=(vmem, vmem),
         scratch_shapes=[
+            pltpu.VMEM(features.shape, jnp.bfloat16),
+            pltpu.VMEM(cotangent.shape, jnp.bfloat16),
+            pltpu.VMEM(weight_in.shape, jnp.bfloat16),
+            pltpu.VMEM(weight_out.shape, jnp.bfloat16),
+            pltpu.SemaphoreType.DMA((4,)),
             pltpu.VMEM((16, wavevectors.shape[1]), jnp.bfloat16),
             pltpu.VMEM((16, atoms), jnp.bfloat16),
             pltpu.VMEM((total_rows, atoms), jnp.bfloat16),
             pltpu.VMEM(block, jnp.float32),
             pltpu.VMEM(block, jnp.bfloat16),
-            pltpu.VMEM(block, jnp.bfloat16),
+            halved, halved, halved,
             pltpu.VMEM((chunks, n, channels, BLOCK), jnp.bfloat16),
             pltpu.VMEM((channels, atoms), jnp.float32),
-        ] + [spread] * 7 + [atom_sems] * 4 + [one_sem] * 2 + [sub_sems] * 6,
+        ] + [spread] * 7 + [chunk_sem] * 4 + [atom_sems] * 4 + [one_sem] * 2 + [sub_sems] * 6,
         compiler_params=pltpu.CompilerParams(
             collective_id=0, has_side_effects=True, vmem_limit_bytes=48 * 2**20
         ),
@@ -322,8 +396,10 @@
 def own_filter(wavevectors, radial_weight, atom_count, n, me):
     kvec = wavevectors.shape[1]
     waves = n * BLOCK // 2
-    chunked = wavevectors.reshape(3, kvec // waves, n // 2, BLOCK)
-    own = lax.dynamic_index_in_dim(chunked, lax.rem(me, n // 2), 2, keepdims=False).reshape(3, -1)
+    own = jnp.concatenate([
+        lax.dynamic_slice_in_dim(wavevectors, j * waves + (me // 2) * BLOCK, BLOCK, 1)
+        for j in range(kvec // waves)
+    ], 1)
     lengths = jnp.sqrt(jnp.sum((own * own).astype(jnp.float32), 0))
     spacing = KMAX * math.sqrt(3.0) / (NB - 1)
     centers = jnp.arange(NB).astype(jnp.float32) * spacing

time: 109 us -> 103 us (0.945); the launches traced: 107 us -> 102 us
  Pallas kernels: 98.4 us -> 93.8 us
    pallas_call x1, Pallas kernels: 98.4 us -> 93.8 us  [layer(): pl.pallas_call(functools.partial(layer_kernel, n, nc, chunks), out_shape=...]
where the time goes in v3:
time: 103 us; the launch traced here: 102 us
  Pallas kernels  93.8 us (91%)
  local copies, waits for them, and re-layouts  7.1 us (7%)
    pallas_call x1, Pallas kernels, layer(): pl.pallas_call(functools.partial(layer_kernel, n, nc, chunks), out_shape=...  93.8 us
    unnamed x16, local copies, waits for them, and re-layouts  7.09 us

profile of v3, /device:TPU:0, one launch (start us, length us, event | category | flops | bytes accessed | tf_op | source)
XLA Modules:
  0.0 102.3 jit_solution(4052975921844506539)
XLA Ops:
  0.6 0.0 copy-start
  0.6 0.0 copy-start.5
  0.7 0.7 copy-done.5
  1.4 0.0 copy-done
  1.5 0.0 copy-start.6
  1.5 0.7 convolution_multiply_fusion.refs_3_
  2.2 0.1 copy-done.6
  2.2 0.0 copy-start.1
  2.2 1.2 %copy-done.1 = bf16[512,1024]{1,0:T(8,128)(2,1)S(1)} copy-done((bf16[512,1024]{1,0:T(8,128)(2,1)S(1)}, bf16[512,1024]{1,0:T(8,128)(2,1)}, u32[]{:S(2)}) %copy-start.1) | copy-done | bytes 1048600
  3.4 0.0 copy-start.2
  3.4 1.2 %copy-done.2 = bf16[1024,512]{1,0:T(8,128)(2,1)S(1)} copy-done((bf16[1024,512]{1,0:T(8,128)(2,1)S(1)}, bf16[1024,512]{1,0:T(8,128)(2,1)}, u32[]{:S(2)}) %copy-start.2) | copy-done | bytes 1048600
  4.7 0.0 copy-start.3
  4.7 1.0 %copy-done.3 = bf16[2048,128]{1,0:T(8,128)(2,1)S(1)} copy-done((bf16[2048,128]{1,0:T(8,128)(2,1)S(1)}, bf16[2048,128]{1,0:T(8,128)(2,1)}, u32[]{:S(2)}) %copy-start.3) | copy-done | bytes 524312
  5.7 0.0 copy-start.4
  5.7 1.0 %copy-done.4 = bf16[2048,128]{1,0:T(8,128)(2,1)S(1)} copy-done((bf16[2048,128]{1,0:T(8,128)(2,1)S(1)}, bf16[2048,128]{1,0:T(8,128)(2,1)}, u32[]{:S(2)}) %copy-start.4) | copy-done | bytes 524312
  6.8 93.8 %layer.1 = (bf16[2048,128]{1,0:T(8,128)(2,1)S(1)}, f32[2048,128]{1,0:T(8,128)S(1)}) custom-call(s32[3,2048]{1,0:T(4,128)S(1)} %copy-done.5, s32[3,2048]{1,0:T(4,128)S(1)} %copy-done.6, bf16[2048,128]{1,0:T(8,128)(2,1)S(1)} %copy-done.3, f32[512,128]{1,0:T(8,128)S(1)} %convolution_multiply_fusion.refs_3_, bf16[512,1024]{1,0:T(8,128)(2,1)S(1)} %copy-done.1, ...), custom_call_target="tpu_custom_call" | custom-call | tf_op jit(solution)/shard_map/layer/pallas_call | solution.py:366
  100.5 0.8 copy.11
  101.3 1.0 copy.12
  (4 shorter events, 0.0 us)
Async XLA Ops:
  0.6 0.8 copy-start
  0.6 0.8 copy-start.5
  1.5 0.8 copy-start.6
  2.2 1.2 %copy-start.1 = (bf16[512,1024]{1,0:T(8,128)(2,1)S(1)}, bf16[512,1024]{1,0:T(8,128)(2,1)}, u32[]{:S(2)}) copy-start(bf16[512,1024]{1,0:T(8,128)(2,1)} %refs_4_.1) | copy-start | bytes 3145732
  3.4 1.2 %copy-start.2 = (bf16[1024,512]{1,0:T(8,128)(2,1)S(1)}, bf16[1024,512]{1,0:T(8,128)(2,1)}, u32[]{:S(2)}) copy-start(bf16[1024,512]{1,0:T(8,128)(2,1)} %refs_5_.1) | copy-start | bytes 3145732
  4.7 1.0 %copy-start.3 = (bf16[2048,128]{1,0:T(8,128)(2,1)S(1)}, bf16[2048,128]{1,0:T(8,128)(2,1)}, u32[]{:S(2)}) copy-start(bf16[2048,128]{1,0:T(8,128)(2,1)} %refs_2_.1) | copy-start | bytes 1572868
  5.7 1.0 %copy-start.4 = (bf16[2048,128]{1,0:T(8,128)(2,1)S(1)}, bf16[2048,128]{1,0:T(8,128)(2,1)}, u32[]{:S(2)}) copy-start(bf16[2048,128]{1,0:T(8,128)(2,1)} %refs_6_.1) | copy-start | bytes 1572868

commit v4 on v3

--- a/solution.py
+++ b/solution.py
@@ -387,7 +387,7 @@
             pltpu.VMEM((channels, atoms), jnp.float32),
         ] + [spread] * 7 + [chunk_sem] * 4 + [atom_sems] * 4 + [one_sem] * 2 + [sub_sems] * 6,
         compiler_params=pltpu.CompilerParams(
-            collective_id=0, has_side_effects=True, vmem_limit_bytes=48 * 2**20
+            collective_id=0, has_side_effects=True, vmem_limit_bytes=61 * 2**20
         ),
         name="layer",
     )(wavevectors, positions, features, filt, weight_in, weight_out, cotangent)

time: 103 us -> 102 us (level)
  local copies, waits for them, and re-layouts: 7.1 us -> 3.69 us
  Pallas kernels: 93.8 us -> 95.6 us
    unnamed x16 -> x6, local copies, waits for them, and re-layouts: 7.09 us -> 2.94 us
    pallas_call x1, Pallas kernels: 93.8 us -> 95.6 us  [layer(): pl.pallas_call(functools.partial(layer_kernel, n, nc, chunks), out_shape=...]
where the time goes in v4:
time: 102 us; the launch traced here: 101 us
  Pallas kernels  95.6 us (94%)
  local copies, waits for them, and re-layouts  3.69 us (4%)
  matrix products  1.38 us (1%)
    pallas_call x1, Pallas kernels, layer(): pl.pallas_call(functools.partial(layer_kernel, n, nc, chunks), out_shape=...  95.6 us
    unnamed x6, local copies, waits for them, and re-layouts  2.94 us

profile of v4, /device:TPU:0, one launch (start us, length us, event | category | flops | bytes accessed | tf_op | source)
XLA Modules:
  0.0 101.4 jit_solution(8424381351041909916)
XLA Ops:
  0.6 0.0 copy-start
  0.7 0.7 constant_dynamic-slice_fusion.3
  1.5 0.0 copy-done
  1.5 1.4 %convolution_multiply_fusion.refs_3_ = f32[512,128]{1,0:T(8,128)} fusion(f32[16,128]{1,0:T(8,128)S(1)} %copy-done, f32[16]{0:T(128)S(1)} %convert_multiply_fusion, f32[512]{0:T(512)S(1)} %sqrt.7), kind=kOutput, calls=%fused_computation | convolution fusion | flops 12681216 | bytes 272448 | tf_op jit(solution)/shard_map/dot_general | solution.py:407
  2.9 95.6 %layer.1 = (bf16[2048,128]{1,0:T(8,128)(2,1)}, f32[2048,128]{1,0:T(8,128)}) custom-call(s32[3,2048]{1,0:T(4,128)} %refs_0_.1, s32[3,2048]{1,0:T(4,128)} %refs_1_.1, bf16[2048,128]{1,0:T(8,128)(2,1)} %refs_2_.1, f32[512,128]{1,0:T(8,128)} %convolution_multiply_fusion.refs_3_, bf16[512,1024]{1,0:T(8,128)(2,1)} %refs_4_.1, bf16[1024,512]{1,0:T(8,128)(2,1)} %refs_5_.1, ...), custom_call_target="tpu_custom_call" | custom-call | tf_op jit(solution)/shard_map/layer/pallas_call | solution.py:366
  98.4 0.0 copy-start.1
  98.4 2.0 %copy.11 = bf16[2048,128]{1,0:T(8,128)(2,1)} copy(bf16[2048,128]{1,0:T(8,128)(2,1)} %get-tuple-element.8) | data formatting | bytes 1048576
  100.4 0.0 copy-done.1
  100.4 1.0 copy.12
  (3 shorter events, 0.0 us)
Async XLA Ops:
  0.6 0.8 copy-start
  98.4 2.0 %copy-start.1 = (f32[2048,128]{1,0:T(8,128)S(1)}, f32[2048,128]{1,0:T(8,128)}, u32[]{:S(2)}) copy-start(f32[2048,128]{1,0:T(8,128)} %get-tuple-element.9) | copy-start | bytes 3145732
